TPU v7x, 32 devices: a whole 2x2x4 slice. The times are simulated.
32 devices in a mesh: dp: 8 (over z, x), tensor: 4 (over y, core).
Axes of the slice: x: 2, y: 2, z: 4, core: 2. Of those that a mesh axis runs over, the one named last changes fastest.
Arguments:
- tokens_in: bfloat16 [16384, 1024], P(('dp', 'tensor')), may hold values from -6 to 6
- doc_ids: int32 [16384], P('dp'), may hold values from 0 to 15, as said below
- gain_mixer: bfloat16 [1024], replicated, may hold values from 0.25 to 1.75
- in_weight: bfloat16 [1024, 3, 1024], P('dp', None, 'tensor'), may hold values from -0.1875 to 0.1875
- conv_weight: bfloat16 [3, 1024], P(None, 'tensor'), may hold values from -3.5 to 3.5
- out_weight: bfloat16 [1024, 1024], P('tensor', 'dp'), may hold values from -0.1875 to 0.1875
- gain_ffn: bfloat16 [1024], replicated, may hold values from 0.25 to 1.75
- gate_up_weight: bfloat16 [1024, 2, 4608], P('dp', None, 'tensor'), may hold values from -0.1875 to 0.1875
- down_weight: bfloat16 [4608, 1024], P('tensor', 'dp'), may hold values from -0.09375 to 0.09375
- cotangent: bfloat16 [16384, 1024], P(('dp', 'tensor')), may hold values from -6 to 6
Outputs:
- block_out: bfloat16 [16384, 1024], P(('dp', 'tensor'))
- grad_input: float32 [16384, 1024], P(('dp', 'tensor'))
- grad_gain_mixer: float32 [1024], replicated
- grad_in_weight: float32 [1024, 3, 1024], P('dp', None, 'tensor')
- grad_conv_weight: float32 [3, 1024], P(None, 'tensor')
- grad_out_weight: float32 [1024, 1024], P('tensor', 'dp')
- grad_gain_ffn: float32 [1024], replicated
- grad_gate_up: float32 [1024, 2, 4608], P('dp', None, 'tensor')
- grad_down: float32 [4608, 1024], P('tensor', 'dp')
Inputs may be any that keep to these rules, and one draw needn't show every extreme that they name: `doc_ids`: document numbers start at 0 at the first token and never fall; each aligned stretch of 1024 tokens after the first holds exactly one document start, never at its first two tokens, and the first stretch holds none.
All inputs are finite; a program needn't handle non-finite values.
Results may differ from a plain program's by a relative error of at most 0.0099.
Values may be sent and summed in bfloat16 or wider, within the bound.
No kernel may reach another device: no remote copies, remote signals or barrier semaphores. Data moves between devices by JAX's collectives and lax.ppermute only.
A program may use at most 192 MiB of HBM per device.

v0:
```python
import jax
import jax.numpy as jnp
from jax import lax
from jax.sharding import PartitionSpec as P

epsilon = 1e-05


def from_behind(shard, axis, by):
    peers = lax.axis_size(axis)
    pairs = [(i, i + by) for i in range(peers) if 0 <= i + by < peers]
    return lax.ppermute(shard, axis, pairs)


def matmul(left, right):
    return jnp.dot(left, right, preferred_element_type=jnp.float32)


def matmul_tn(left, right):
    return lax.dot_general(
        left, right, (((0,), (0,)), ((), ())), preferred_element_type=jnp.float32
    )


def matmul_nt(left, right):
    return lax.dot_general(
        left, right, (((1,), (1,)), ((), ())), preferred_element_type=jnp.float32
    )


def normalize(values):
    scale_vec = lax.rsqrt(jnp.mean(values * values, axis=-1, keepdims=True) + epsilon)
    return (values * scale_vec, scale_vec)


def norm_back(d_normed, normed, scale_vec):
    return scale_vec * (d_normed - normed * jnp.mean(d_normed * normed, axis=-1, keepdims=True))


def body(
    tokens_in,
    doc_ids,
    gain_mixer,
    in_weight,
    conv_weight,
    out_weight,
    gain_ffn,
    gate_up_weight,
    down_weight,
    cotangent,
):
    model_width = tokens_in.shape[1]
    w_in, w_out, w_gu, w_down = (
        lax.all_gather(in_weight, "dp", axis=0, tiled=True),
        lax.all_gather(out_weight, "dp", axis=1, tiled=True),
        lax.all_gather(gate_up_weight, "dp", axis=0, tiled=True),
        lax.all_gather(down_weight, "dp", axis=1, tiled=True),
    )
    channels = w_in.shape[2]
    unit_count = w_gu.shape[2]
    w_in_flat = w_in.reshape(model_width, 3 * channels)
    w_gu_flat = w_gu.reshape(model_width, 2 * unit_count)
    tokens_f = tokens_in.astype(jnp.float32)
    gain_one = gain_mixer.astype(jnp.float32)
    gain_two = gain_ffn.astype(jnp.float32)
    taps = conv_weight.astype(jnp.float32)
    normed_one, scale_one = normalize(tokens_f)
    hidden_one = (normed_one * gain_one).astype(jnp.bfloat16)
    hidden_full = lax.all_gather(hidden_one, "tensor", axis=0, tiled=True)
    group_rows = hidden_full.shape[0]
    projected = matmul(hidden_full, w_in_flat)
    b_part = projected[:, :channels]
    c_part = projected[:, channels : 2 * channels]
    v_part = projected[:, 2 * channels :]
    gated_bx = b_part * v_part
    prev_rim = from_behind(gated_bx[group_rows - 2 :], "dp", 1)
    extended = jnp.concatenate([prev_rim, gated_bx], axis=0)
    ids_ext = jnp.concatenate([doc_ids[:1], doc_ids[:1], doc_ids], axis=0)
    keep_one = (ids_ext[1:-1] == ids_ext[2:]).astype(jnp.float32)[:, None]
    keep_two = (ids_ext[:-2] == ids_ext[2:]).astype(jnp.float32)[:, None]
    conv_out = (
        taps[0] * gated_bx
        + taps[1] * keep_one * extended[1:-1]
        + taps[2] * keep_two * extended[:-2]
    )
    gated = (c_part * conv_out).astype(jnp.bfloat16)
    mixed = lax.psum_scatter(matmul(gated, w_out), "tensor", scatter_dimension=0, tiled=True)
    resid = tokens_f + mixed
    normed_two, scale_two = normalize(resid)
    hidden_two = (normed_two * gain_two).astype(jnp.bfloat16)
    second_full = lax.all_gather(hidden_two, "tensor", axis=0, tiled=True)
    gate_up = matmul(second_full, w_gu_flat)
    gate_part = gate_up[:, :unit_count]
    up_part = gate_up[:, unit_count:]
    sigma_gate = jax.nn.sigmoid(gate_part)
    silu_gate = gate_part * sigma_gate
    activated = (silu_gate * up_part).astype(jnp.bfloat16)
    ffn_rows_out = lax.psum_scatter(
        matmul(activated, w_down).astype(jnp.bfloat16), "tensor", scatter_dimension=0, tiled=True
    ).astype(jnp.float32)
    block_out = (resid + ffn_rows_out).astype(jnp.bfloat16)
    cot_full = lax.all_gather(cotangent, "tensor", axis=0, tiled=True)
    grad_down_part = matmul_tn(activated, cot_full)
    d_act = matmul_nt(cot_full, w_down)
    d_gate = d_act * up_part * sigma_gate * (1.0 + gate_part * (1.0 - sigma_gate))
    d_up = d_act * silu_gate
    d_gu = jnp.concatenate([d_gate, d_up], axis=1).astype(jnp.bfloat16)
    grad_gu_part = matmul_tn(second_full, d_gu).reshape(model_width, 2, unit_count)
    d_hidden_two = lax.psum_scatter(
        matmul_nt(d_gu, w_gu_flat), "tensor", scatter_dimension=0, tiled=True
    )
    part_gain_two = jnp.sum(d_hidden_two * normed_two, axis=0)
    d_resid = cotangent.astype(jnp.float32) + norm_back(
        d_hidden_two * gain_two, normed_two, scale_two
    )
    d_mix = d_resid.astype(jnp.bfloat16)
    mix_full = lax.all_gather(d_mix, "tensor", axis=0, tiled=True)
    grad_out_part = matmul_tn(gated, mix_full)
    d_gated = matmul_nt(mix_full, w_out)
    d_conv = d_gated * c_part
    d_c_part = d_gated * conv_out
    edge_one = keep_one * d_conv
    edge_two = keep_two * d_conv
    next_rim = from_behind(jnp.stack([edge_one[:2], edge_two[:2]]), "dp", -1)
    edge_one_ext = jnp.concatenate([edge_one, next_rim[0]], axis=0)
    edge_two_ext = jnp.concatenate([edge_two, next_rim[1]], axis=0)
    d_bx = (
        taps[0] * d_conv + taps[1] * edge_one_ext[1 : group_rows + 1] + taps[2] * edge_two_ext[2:]
    )
    conv_local = jnp.stack(
        [
            jnp.sum(gated_bx * d_conv, axis=0),
            jnp.sum(extended[1:-1] * edge_one, axis=0),
            jnp.sum(extended[:-2] * edge_two, axis=0),
        ]
    )
    d_proj = jnp.concatenate([d_bx * v_part, d_c_part, d_bx * b_part], axis=1).astype(jnp.bfloat16)
    grad_in_part = matmul_tn(hidden_full, d_proj).reshape(model_width, 3, channels)
    d_hidden_one = lax.psum_scatter(
        matmul_nt(d_proj, w_in_flat), "tensor", scatter_dimension=0, tiled=True
    )
    part_gain_one = jnp.sum(d_hidden_one * normed_one, axis=0)
    grad_input = d_resid + norm_back(d_hidden_one * gain_one, normed_one, scale_one)
    offset = lax.axis_index("tensor") * channels
    zero_index = jnp.zeros((), jnp.int32)
    conv_spread = lax.dynamic_update_slice(
        jnp.zeros((conv_local.shape[0], model_width), jnp.float32), conv_local, (zero_index, offset)
    )
    gain_one_sum, gain_two_sum, conv_sum = lax.psum(
        (part_gain_one, part_gain_two, conv_spread), ("dp", "tensor")
    )
    grad_conv = lax.dynamic_slice(conv_sum, (zero_index, offset), (conv_local.shape[0], channels))
    grad_in, grad_out, grad_gu, grad_down = (
        lax.psum_scatter(grad_in_part, "dp", scatter_dimension=0, tiled=True),
        lax.psum_scatter(grad_out_part, "dp", scatter_dimension=1, tiled=True),
        lax.psum_scatter(grad_gu_part, "dp", scatter_dimension=0, tiled=True),
        lax.psum_scatter(grad_down_part, "dp", scatter_dimension=1, tiled=True),
    )
    return (
        block_out,
        grad_input,
        gain_one_sum,
        grad_in,
        grad_conv,
        grad_out,
        gain_two_sum,
        grad_gu,
        grad_down,
    )


def solution(mesh):
    return jax.shard_map(
        body,
        mesh=mesh,
        in_specs=(
            P(("dp", "tensor"), None),
            P("dp"),
            P(),
            P("dp", None, "tensor"),
            P(None, "tensor"),
            P("tensor", "dp"),
            P(),
            P("dp", None, "tensor"),
            P("tensor", "dp"),
            P(("dp", "tensor"), None),
        ),
        out_specs=(
            P(("dp", "tensor"), None),
            P(("dp", "tensor"), None),
            P(),
            P("dp", None, "tensor"),
            P(None, "tensor"),
            P("tensor", "dp"),
            P(),
            P("dp", None, "tensor"),
            P("tensor", "dp"),
        ),
        check_vma=False,
    )
```

profile of v0, /device:TPU:0, one launch (start us, length us, event | category | flops | bytes accessed | tf_op | source)
XLA Modules:
  0.0 1216.5 jit_solution(15998534206006718899)
XLA Ops:
  7.2 1.8 copy.26
  9.8 1.5 fusion.14
  11.4 1.3 fusion.8
  13.3 1.4 concatenate.25
  15.4 33.0 %all_gather.26 = bf16[256,1024]{1,0:T(8,128)(2,1)} all-gather(bf16[256,128]{1,0:T(8,128)(2,1)S(1)} %copy-done.13), channel_id=1, replica_groups=mesh['dp'=8,'tensor'=4] {'dp'}, dimensions={1}, use_global_device_ids=true | all-gather | bytes 589824 | tf_op jit(solution)/shard_map/all_gather | solution.py:55
  48.4 13.8 %all-gather.10.cloned.1.call-done = bf16[1024,3,256]{0,2,1:T(8,128)(2,1)} async-done(((bf16[128,3,256]{0,2,1:T(8,128)(2,1)}), bf16[1024,3,256]{0,2,1:T(8,128)(2,1)}) %all-gather.10.cloned.1.call-update) | async-done | bytes 1572880 | tf_op jit(solution)/shard_map/all_gather | solution.py:54
  62.2 35.4 %all-gather.8.cloned.1.call-done = bf16[2048,1024]{1,0:T(8,128)(2,1)} async-done(((bf16[512,1024]{1,0:T(8,128)(2,1)}), bf16[2048,1024]{1,0:T(8,128)(2,1)}) %all-gather.8.cloned.1.call-update) | async-done | bytes 4194320 | tf_op jit(solution)/shard_map/all_gather | solution.py:69
  97.6 5.7 fusion.31
  103.6 3.4 collective-permute-start
  107.0 1.3 collective-permute-done
  108.3 2.0 multiply_convert_fusion.7
  111.3 4.5 fusion.32
  116.5 72.0 %reduce-scatter.8.cloned.1.call-done = f32[512,1024]{1,0:T(8,128)} async-done(((f32[2048,1024]{1,0:T(8,128)}), f32[512,1024]{1,0:T(8,128)}) %reduce-scatter.8.cloned.1.call-update) | async-done | bytes 2097168 | tf_op jit(solution)/shard_map/reduce_scatter | solution.py:87
  188.6 1.9 multiply_reduce_fusion.5
  193.3 77.4 %all-gather.14.cloned.1.call-done = bf16[1024,2,1152]{2,1,0:T(2,128)(2,1)} async-done(((bf16[128,2,1152]{2,1,0:T(2,128)(2,1)}), bf16[1024,2,1152]{2,1,0:T(2,128)(2,1)}) %all-gather.14.cloned.1.call-update) | async-done | bytes 4718608 | tf_op jit(solution)/shard_map/all_gather | solution.py:56
  270.7 5.3 copy.31
  276.0 29.4 %all-gather.12.cloned.1.call-done = bf16[2048,1024]{1,0:T(8,128)(2,1)} async-done(((bf16[512,1024]{1,0:T(8,128)(2,1)}), bf16[2048,1024]{1,0:T(8,128)(2,1)}) %all-gather.12.cloned.1.call-update) | async-done | bytes 4194320 | tf_op jit(solution)/shard_map/all_gather | solution.py:91
  305.5 16.7 %fusion.33 = f32[2048,2304]{1,0:T(8,128)} fusion(bf16[2048,1024]{1,0:T(8,128)(2,1)} %all-gather.12.cloned.1.call-done, bf16[1024,2304]{1,0:T(8,128)(2,1)} %bitcast.42), kind=kOutput, calls=%fused_computation.79 | convolution fusion | flops 9663676416 | bytes 27787264 | tf_op jit(solution)/shard_map/dot_general | solution.py:16
  322.2 39.2 %all-gather.16.cloned.1.call-done = bf16[1152,1024]{1,0:T(8,128)(2,1)} async-done(((bf16[1152,128]{1,0:T(8,128)(2,1)}), bf16[1152,1024]{1,0:T(8,128)(2,1)}) %all-gather.16.cloned.1.call-update) | async-done | bytes 2359312 | tf_op jit(solution)/shard_map/all_gather | solution.py:57
  361.3 34.3 %all-gather.18.cloned.1.call-done = bf16[2048,1024]{1,0:T(8,128)(2,1)} async-done(((bf16[512,1024]{1,0:T(8,128)(2,1)}), bf16[2048,1024]{1,0:T(8,128)(2,1)}) %all-gather.18.cloned.1.call-update) | async-done | bytes 4194320 | tf_op jit(solution)/shard_map/all_gather | solution.py:102
  395.7 18.4 %multiply_convert_fusion.1 = (bf16[2048,1152]{1,0:T(8,128)(2,1)}, bf16[2048,1152]{1,0:T(8,128)(2,1)}, bf16[2048,1152]{1,0:T(8,128)(2,1)}) fusion(f32[2048,2304]{1,0:T(8,128)} %fusion.33, bf16[2048,1024]{1,0:T(8,128)(2,1)} %all-gather.18.cloned.1.call-done, bf16[1152,1024]{1,0:T(8,128)(2,1)} %all-gather.16.cloned.1.call-done), kind=kOutput, calls=%fused_computation.2 | convolution fusion | flops 4867227648 | bytes 39583744 | tf_op jit(solution)/shard_map/dot_general | solution.py:26
  414.1 15.9 %fusion.2 = f32[2048,1024]{1,0:T(8,128)} fusion(bf16[1024,2304]{1,0:T(8,128)(2,1)} %bitcast.43, bf16[2048,1152]{1,0:T(8,128)(2,1)} %get-tuple-element.29, bf16[2048,1152]{1,0:T(8,128)(2,1)} %get-tuple-element.28), kind=kOutput, calls=%fused_computation.7 | convolution fusion | flops 9682550784 | bytes 22544384 | tf_op jit(solution)/shard_map/dot_general | solution.py:26
  430.3 71.6 %reduce-scatter.12.cloned.1.call-done = f32[512,1024]{1,0:T(8,128)} async-done(((f32[2048,1024]{1,0:T(8,128)}), f32[512,1024]{1,0:T(8,128)}) %reduce-scatter.12.cloned.1.call-update) | async-done | bytes 2097168 | tf_op jit(solution)/shard_map/reduce_scatter | solution.py:109
  501.9 2.3 multiply_reduce_fusion
  504.4 1.6 fusion.28
  506.0 16.7 %fusion.1 = f32[1024,2304]{1,0:T(8,128)} fusion(bf16[2048,1024]{1,0:T(8,128)(2,1)} %all-gather.12.cloned.1.call-done, bf16[2048,1152]{1,0:T(8,128)(2,1)} %get-tuple-element.29, bf16[2048,1152]{1,0:T(8,128)(2,1)} %get-tuple-element.28), kind=kOutput, calls=%fused_computation.6 | convolution fusion | flops 9682550784 | bytes 23068672 | tf_op jit(solution)/shard_map/dot_general | solution.py:20
  522.8 11.9 reshape.61
  534.8 5.9 all-gather.20.cloned.1.call-done
  540.6 3.8 fusion.34
  544.5 3.9 multiply_reduce_fusion.2
  548.4 1.3 collective-permute-start.1
  549.7 4.3 collective-permute-done.1
  556.9 5.7 fusion.20
  562.9 9.5 convolution_convert_fusion
  572.4 9.7 fusion.36
  582.2 4.9 fusion.35
  587.2 8.3 fusion.19
  595.5 3.6 copy.29
  601.0 241.5 %all-reduce.4.cloned.1.call-done = f32[1024,2,1152]{2,1,0:T(2,128)} async-done(((f32[1024,2,1152]{2,1,0:T(2,128)}), f32[1024,2,1152]{2,1,0:T(2,128)}) %all-reduce.4.cloned.1.call-update) | async-done | bytes 9437200
  842.5 2.4 constant_dynamic-slice_fusion
  844.9 70.9 %reduce-scatter.14.cloned.1.call-done = f32[512,1024]{1,0:T(8,128)} async-done(((f32[2048,1024]{1,0:T(8,128)}), f32[512,1024]{1,0:T(8,128)}) %reduce-scatter.14.cloned.1.call-update) | async-done | bytes 2097168 | tf_op jit(solution)/shard_map/reduce_scatter | solution.py:139
  915.9 2.3 fusion.13
  918.1 40.1 %all-reduce.1 = (f32[1024]{0:T(1024)}, f32[3,1024]{1,0:T(4,128)S(1)}, f32[1024]{0:T(1024)}) all-reduce(f32[1024]{0:T(1024)S(1)} %get-tuple-element.11, f32[3,1024]{1,0:T(4,128)S(1)} %maximum_dynamic-update-slice_fusion, f32[1024]{0:T(1024)S(1)} %get-tuple-element.9), channel_id=1, replica_groups=mesh['dp'=8,'tensor'=4] {'dp','tensor'}, use_global_device_ids=true, to_apply=%region_9.0 | all-reduce | flops 5120 | bytes 40960 | tf_op jit(solution)/shard_map/psum | solution.py:149
  958.9 4.8 reduce-scatter.10.cloned.1.call-done
  963.7 4.5 fusion.12
  968.2 95.4 %reduce-scatter.20.cloned.1.call-done = f32[1152,128]{1,0:T(8,128)} async-done(((f32[1152,1024]{1,0:T(8,128)}), f32[1152,128]{1,0:T(8,128)}) %reduce-scatter.20.cloned.1.call-update) | async-done | bytes 589840 | tf_op jit(solution)/shard_map/reduce_scatter | solution.py:157
  1063.6 67.6 %reduce-scatter.18.cloned.1.call-done = f32[256,128]{1,0:T(8,128)} async-done(((f32[256,1024]{1,0:T(8,128)}), f32[256,128]{1,0:T(8,128)}) %reduce-scatter.18.cloned.1.call-update) | async-done | bytes 131088 | tf_op jit(solution)/shard_map/reduce_scatter | solution.py:155
  1131.1 78.4 %reduce-scatter.16.cloned.1.call-done = f32[128,3,256]{2,0,1:T(8,128)} async-done(((f32[1024,3,256]{2,0,1:T(8,128)}), f32[128,3,256]{2,0,1:T(8,128)}) %reduce-scatter.16.cloned.1.call-update) | async-done | bytes 393232 | tf_op jit(solution)/shard_map/reduce_scatter | solution.py:154
  (98 shorter events, 12.6 us)
Async XLA Ops:
  7.2 4.2 copy-start
  7.2 55.0 %all-gather.10.cloned.1.call-start = ((), (), s32[]{:S(2)}) async-start(), calls=%async_computation.8 | async-start | bytes 1769472 | tf_op jit(solution)/shard_map/all_gather | solution.py:54
  9.1 88.5 %all-gather.8.cloned.1.call-start = ((), (), s32[]{:S(2)}) async-start(), calls=%async_computation.7 | async-start | bytes 5242880 | tf_op jit(solution)/shard_map/all_gather | solution.py:69
  9.8 2.9 copy-start.11
  9.8 2.9 copy-start.16
  9.8 5.6 copy-start.13
  11.4 1.4 copy-start.14
  12.7 175.9 %reduce-scatter.8.cloned.1.call-start = ((), (), s32[]{:S(2)}) async-start(), calls=%async_computation.9 | async-start | bytes 10485760 | tf_op jit(solution)/shard_map/reduce_scatter | solution.py:87
  103.3 5.0 copy-start.1
  103.3 3.7 copy-start.17
  103.6 6.7 copy-start.2
  103.6 4.7 collective-permute-start
  108.3 3.0 copy-start.7
  110.3 1.0 copy-start.6
  115.8 0.7 copy-start.18
  115.9 154.9 %all-gather.14.cloned.1.call-start = ((), (), s32[]{:S(2)}) async-start(), calls=%async_computation.11 | async-start | bytes 5308416 | tf_op jit(solution)/shard_map/all_gather | solution.py:56
  116.5 189.0 %all-gather.12.cloned.1.call-start = ((), (), s32[]{:S(2)}) async-start(), calls=%async_computation.10 | async-start | bytes 5242880 | tf_op jit(solution)/shard_map/all_gather | solution.py:91
  191.8 169.6 %all-gather.16.cloned.1.call-start = ((), (), s32[]{:S(2)}) async-start(), calls=%async_computation.12 | async-start | bytes 2654208 | tf_op jit(solution)/shard_map/all_gather | solution.py:57
  192.3 203.4 %all-gather.18.cloned.1.call-start = ((), (), s32[]{:S(2)}) async-start(), calls=%async_computation.14 | async-start | bytes 5242880 | tf_op jit(solution)/shard_map/all_gather | solution.py:102
  193.1 308.8 %reduce-scatter.12.cloned.1.call-start = ((), (), s32[]{:S(2)}) async-start(), calls=%async_computation.15 | async-start | bytes 10485760 | tf_op jit(solution)/shard_map/reduce_scatter | solution.py:109
  430.0 110.6 %all-gather.20.cloned.1.call-start = ((), (), s32[]{:S(2)}) async-start(), calls=%async_computation.16 | async-start | bytes 5242880 | tf_op jit(solution)/shard_map/all_gather | solution.py:117
  501.9 2.3 copy-start.4
  501.9 2.5 copy-start.5
  506.0 336.5 %all-reduce.4.cloned.1.call-start = ((), (), s32[]{:S(2)}) async-start(), calls=%async_computation.21 | async-start | bytes 18874368
  534.7 381.1 %reduce-scatter.14.cloned.1.call-start = ((), (), s32[]{:S(2)}) async-start(), calls=%async_computation.17 | async-start | bytes 10485760 | tf_op jit(solution)/shard_map/reduce_scatter | solution.py:139
  540.6 3.8 copy-start.3
  540.6 13.3 %slice-start = ((s8[6291456]{0:T(1024)(128)(4,1)}), s8[4194304]{0:T(1024)(128)(4,1)S(1)}, s32[]{:S(2)}) async-start(s8[6291456]{0:T(1024)(128)(4,1)} %bitcast.39), calls=%async_computation.22 | async-start | bytes 8388608
  544.4 9.5 slice-start.1
  548.3 6.8 copy-start.10
  548.4 5.6 collective-permute-start.1
  554.7 1.0 copy-start.8
  554.7 2.2 copy-start.19
  555.1 1.0 copy-start.9
  562.6 401.1 %reduce-scatter.10.cloned.1.call-start = ((), (), s32[]{:S(2)}) async-start(), calls=%async_computation.13 | async-start | bytes 5242880 | tf_op jit(solution)/shard_map/reduce_scatter | solution.py:98
  572.4 491.2 %reduce-scatter.20.cloned.1.call-start = ((), (), s32[]{:S(2)}) async-start(), calls=%async_computation.20 | async-start | bytes 5308416 | tf_op jit(solution)/shard_map/reduce_scatter | solution.py:157
  582.2 548.9 %reduce-scatter.18.cloned.1.call-start = ((), (), s32[]{:S(2)}) async-start(), calls=%async_computation.19 | async-start | bytes 1179648 | tf_op jit(solution)/shard_map/reduce_scatter | solution.py:155
  587.1 622.4 %reduce-scatter.16.cloned.1.call-start = ((), (), s32[]{:S(2)}) async-start(), calls=%async_computation.18 | async-start | bytes 3538944 | tf_op jit(solution)/shard_map/reduce_scatter | solution.py:154
  599.1 0.7 copy-start.20
  599.1 316.7 %copy-start.12 = (f32[1024]{0:T(1024)S(1)}, f32[1024]{0:T(1024)}, u32[]{:S(2)}) copy-start(f32[1024]{0:T(1024)} %copy-done.11) | copy-start | bytes 12292
  599.1 316.7 %copy-start.15 = (f32[512]{0:T(512)S(1)}, f32[512]{0:T(512)}, u32[]{:S(2)}) copy-start(f32[512]{0:T(512)} %copy-done.14) | copy-start | bytes 6148
Sparse Core Ops, SparseCore 0:
  10.6 51.5 all-gather.9
  64.3 33.1 all-gather.7
  116.0 72.5 reduce-scatter.7
  190.8 79.8 all-gather.13
  272.8 32.6 all-gather.11
  307.6 53.7 all-gather.15
  363.0 32.6 all-gather.17
  430.2 71.6 reduce-scatter.11
  506.1 34.4 all-gather.19
  544.3 298.1 all-reduce.3
  845.1 70.7 reduce-scatter.13
  918.4 45.2 reduce-scatter.9
  967.9 95.6 reduce-scatter.19
  1067.4 63.6 reduce-scatter.17
  1135.6 73.8 reduce-scatter.15
where the time goes:
time: 1220 us
  waiting for transfers between devices  945 us (77%)
  matrix products  120 us (10%)
  blocking collectives  73.2 us (6%)
  local copies, waits for them, and re-layouts  31.7 us (3%)
  other arithmetic  25.4 us (2%)
  between operations  15.3 us (1%)
    unnamed x16, waiting for transfers between devices  243 us
    reduce_scatter x1, waiting for transfers between devices, body(): lax.psum_scatter(grad_down_part, 'dp', scatter_dimension=1, tiled=True)  95.4 us
    reduce_scatter x1, waiting for transfers between devices, body(): lax.psum_scatter(grad_in_part, 'dp', scatter_dimension=0, tiled=True)  78.4 us
    all_gather x1, waiting for transfers between devices, body(): lax.all_gather(gate_up_weight, 'dp', axis=0, tiled=True)  77.4 us
    reduce_scatter x1, waiting for transfers between devices, body(): lax.psum_scatter(matmul(gated, w_out), 'tensor', scatter_dimension=0, til...  72 us
    reduce_scatter x1, waiting for transfers between devices, body(): lax.psum_scatter(matmul_nt(d_gu, w_gu_flat), 'tensor', scatter_dimension=...  71.6 us
    reduce_scatter x1, waiting for transfers between devices, body(): lax.psum_scatter(matmul_nt(d_proj, w_in_flat), 'tensor', scatter_dimensio...  70.9 us
    reduce_scatter x1, waiting for transfers between devices, body(): lax.psum_scatter(grad_out_part, 'dp', scatter_dimension=1, tiled=True)  67.6 us
  transfers between devices with their start and end apart: 17, of which 17 were waited for; matrix products, arithmetic and copies ran while one was open for 10% of the time, Pallas kernels for 0%

commit v1 on v0

v1 whole, which is shorter than its diff:
```python
import jax
import jax.numpy as jnp
from jax import lax
from jax.experimental import pallas as pl
from jax.experimental.pallas import tpu as pltpu
from jax.sharding import PartitionSpec as P

epsilon = 1e-05
HALO = 16
BF = jnp.bfloat16
F32 = jnp.float32


def swap(value, axis, bit):
    peers = lax.axis_size(axis)
    return lax.ppermute(value, axis, [(i, i ^ bit) for i in range(peers)])


def ring(value, axis, by):
    peers = lax.axis_size(axis)
    return lax.ppermute(value, axis, [(i, (i + by) % peers) for i in range(peers)])


def shift(value, by):
    peers = lax.axis_size("dp") * lax.axis_size("tensor")
    pairs = [(i, i + by) for i in range(peers) if 0 <= i + by < peers]
    return lax.ppermute(value, ("dp", "tensor"), pairs)


def nn(left, right):
    return jnp.dot(left, right, preferred_element_type=F32)


def tn(left, right):
    return lax.dot_general(left, right, (((0,), (0,)), ((), ())), preferred_element_type=F32)


def nt(left, right):
    return lax.dot_general(left, right, (((1,), (1,)), ((), ())), preferred_element_type=F32)


def normalize(values):
    scale_vec = lax.rsqrt(jnp.mean(values * values, axis=-1, keepdims=True) + epsilon)
    return (values * scale_vec, scale_vec)


def norm_back(d_normed, normed, scale_vec):
    return scale_vec * (d_normed - normed * jnp.mean(d_normed * normed, axis=-1, keepdims=True))


def reorder(value, order, width):
    rows, columns = value.shape
    if width % 128:
        return value.reshape(rows, -1, width)[:, order].reshape(rows, columns)

    def copy(order_ref, in_ref, out_ref):
        out_ref[...] = in_ref[...]

    return pl.pallas_call(
        copy,
        out_shape=jax.ShapeDtypeStruct(value.shape, value.dtype),
        grid_spec=pltpu.PrefetchScalarGridSpec(
            num_scalar_prefetch=1,
            grid=(columns // width,),
            in_specs=[pl.BlockSpec((rows, width), lambda i, order_ref: (0, order_ref[i]))],
            out_specs=pl.BlockSpec((rows, width), lambda i, order_ref: (0, i)),
        ),
    )(order, value)


def gather_rows(shard):
    pieces = [shard]
    for _ in range(lax.axis_size("dp") // 2 - 1):
        pieces.append(ring(pieces[-1], "dp", 2))
    half = len(pieces) // 2
    near = jnp.concatenate(pieces[:half], axis=0)
    far = jnp.concatenate(pieces[half:], axis=0)
    return [near, far, swap(near, "dp", 1), swap(far, "dp", 1)]


def scatter_rows(total):
    steps = lax.axis_size("dp") // 2
    rows = total.shape[0] // (2 * steps)
    half = steps * rows
    got = swap(total[half:], "dp", 1)

    def part(k):
        return total[k * rows : (k + 1) * rows].astype(F32) + got[k * rows : (k + 1) * rows].astype(F32)

    run = part(steps - 1)
    for k in range(steps - 2, -1, -1):
        run = ring(run.astype(BF), "dp", -2).astype(F32) + part(k)
    return run


def gather_tokens(own):
    other = swap(own, "tensor", 2)
    return jnp.concatenate([own, swap(own, "tensor", 1), other, swap(other, "tensor", 1)], axis=0)


def scatter_tokens(total, rows):
    low = total.astype(BF)
    got_one = swap(low[rows : 2 * rows], "tensor", 1)
    got_three = swap(low[3 * rows :], "tensor", 1)
    far = total[2 * rows : 3 * rows] + got_three.astype(F32)
    got = swap(far.astype(BF), "tensor", 2)
    return total[:rows] + got_one.astype(F32) + got.astype(F32)


def by_xor(groups, me):
    one = jnp.where((me & 1) == 1, groups[jnp.array([1, 0, 3, 2])], groups)
    return jnp.where((me & 2) == 2, one[jnp.array([2, 3, 0, 1])], one)


def sum_all(value):
    for axis in ("tensor", "dp"):
        bit = 1
        while bit < lax.axis_size(axis):
            value = value + swap(value, axis, bit)
            bit *= 2
    return value


def body(
    tokens_in,
    doc_ids,
    gain_mixer,
    in_weight,
    conv_weight,
    out_weight,
    gain_ffn,
    gate_up_weight,
    down_weight,
    cotangent,
):
    rows, width = tokens_in.shape
    dp_count = lax.axis_size("dp")
    block = width // dp_count
    channels = in_weight.shape[2]
    units = gate_up_weight.shape[2]
    me_dp, me_t = lax.axis_index("dp"), lax.axis_index("tensor")
    deep = dp_count // 2
    my_z, my_x = me_dp // 2, me_dp % 2
    index = jnp.arange(dp_count, dtype=jnp.int32)
    order = ((my_z - index % deep) % deep) * 2 + (my_x ^ (index // deep))
    inverse = (my_x ^ (index % 2)) * deep + (my_z - index // 2) % deep

    packed = jnp.concatenate([in_weight.reshape(block, 3 * channels), out_weight.T], axis=1)
    taps_rows = jnp.zeros((HALO, 4 * channels), BF).at[:3, :channels].set(conv_weight)
    mix_own = jnp.concatenate(gather_rows(packed) + [taps_rows], axis=0)
    mix_y = swap(mix_own, "tensor", 2)
    mix = [mix_own, swap(mix_own, "tensor", 1), mix_y, swap(mix_y, "tensor", 1)]
    cut = units // 2 // 128 * 128
    bounds = [(0, cut), (cut, units)]
    ffn = []
    for lo, hi in bounds:
        shard = jnp.concatenate(
            [gate_up_weight[:, 0, lo:hi], gate_up_weight[:, 1, lo:hi], down_weight[lo:hi].T], axis=1
        )
        ffn.append(jnp.concatenate(gather_rows(shard), axis=0))

    last = doc_ids.shape[0]
    ids = jnp.concatenate([doc_ids[:1], doc_ids[:1], doc_ids, doc_ids[last - 1 :], doc_ids[last - 1 :]])
    ids = lax.dynamic_slice(ids, (me_t * rows,), (rows + 4,))
    one_all = (ids[1:] == ids[:-1]).astype(F32)[:, None]
    two_all = (ids[2:] == ids[:-2]).astype(F32)[:, None]
    keep_one, keep_two = one_all[1 : rows + 1], two_all[:rows]
    next_one, next_two = one_all[2 : rows + 2], two_all[2 : rows + 2]
    tail = tokens_in[rows - HALO :]
    linked = (ids[rows] == ids[rows + 1]).astype(BF)
    tail = tail * jnp.ones((HALO, 1), BF).at[HALO - 2, 0].set(linked)
    extended = jnp.concatenate([shift(tail, 1), tokens_in], axis=0)
    extended = reorder(extended, order, block)
    cot = reorder(cotangent, order, block)
    gains = reorder(jnp.stack([gain_mixer, gain_ffn]), order, block).astype(F32)
    gain_one, gain_two = gains[:1], gains[1:]
    cot_full = gather_tokens(cot)

    normed_ext, scale_ext = normalize(extended.astype(F32))
    hidden_ext = (normed_ext * gain_one).astype(BF)
    normed_one, scale_one = normed_ext[HALO:], scale_ext[HALO:]
    hidden_one = hidden_ext[HALO:]
    tokens_f = extended[HALO:].astype(F32)

    saved = []
    mixed = tokens_f
    for group in mix:
        taps = group[width : width + 3, :channels].astype(F32)
        projected = nn(hidden_ext, group[:width, : 3 * channels])
        b_part = projected[:, :channels]
        c_part = projected[HALO:, channels : 2 * channels]
        v_part = projected[:, 2 * channels :]
        bx = b_part * v_part
        bx0, bx1, bx2 = bx[HALO:], keep_one * bx[HALO - 1 : -1], keep_two * bx[HALO - 2 : -2]
        conv_out = taps[0] * bx0 + taps[1] * bx1 + taps[2] * bx2
        gated = (c_part * conv_out).astype(BF)
        mixed = mixed + nt(gated, group[:width, 3 * channels :])
        saved.append((b_part[HALO:], c_part, v_part[HALO:], bx0, bx1, bx2, conv_out, gated, taps))
    resid = mixed
    normed_two, scale_two = normalize(resid)
    hidden_two = (normed_two * gain_two).astype(BF)
    hidden_full = gather_tokens(hidden_two)

    out_sum = d_sum = 0.0
    ffn_grads = []
    for weights, (lo, hi) in zip(ffn, bounds):
        size = hi - lo
        w_gu, w_down = weights[:, : 2 * size], weights[:, 2 * size :]
        gate_up = nn(hidden_full, w_gu)
        d_act = nn(cot_full, w_down)
        gate, up = gate_up[:, :size], gate_up[:, size:]
        sigma = jax.nn.sigmoid(gate)
        silu = gate * sigma
        act = (silu * up).astype(BF)
        d_gate = d_act * up * sigma * (1.0 + gate * (1.0 - sigma))
        d_gu = jnp.concatenate([d_gate, d_act * silu], axis=1).astype(BF)
        d_sum = d_sum + nt(d_gu, w_gu)
        out_sum = out_sum + nt(act, w_down)
        grads = jnp.concatenate(
            [tn(hidden_full, d_gu).astype(BF), tn(cot_full, act).astype(BF)], axis=1
        )
        ffn_grads.append(scatter_rows(grads))
    d_hidden_two = scatter_tokens(d_sum, rows)
    block_out = reorder((resid + scatter_tokens(out_sum, rows)).astype(BF), inverse, block)

    part_gain_two = jnp.sum(d_hidden_two * normed_two, axis=0)
    d_resid = cot.astype(F32) + norm_back(d_hidden_two * gain_two, normed_two, scale_two)
    d_mix = d_resid.astype(BF)

    d_gated = [nn(d_mix, group[:width, 3 * channels :]) for group in mix]
    d_conv = [back * keep[1] for back, keep in zip(d_gated, saved)]
    first = by_xor(jnp.stack([value[:2] for value in d_conv]), me_t)
    following = by_xor(shift(first, -1), me_t)
    d_hidden_one = 0.0
    conv_parts, mix_grads = [], []
    for r, group in enumerate(mix):
        b_part, c_part, v_part, bx0, bx1, bx2, conv_out, gated, taps = saved[r]
        conv_parts.append(jnp.stack([jnp.sum(v * d_conv[r], axis=0) for v in (bx0, bx1, bx2)]))
        ahead = jnp.concatenate([d_conv[r], following[r]], axis=0)
        d_bx = (
            taps[0] * d_conv[r]
            + taps[1] * next_one * ahead[1 : rows + 1]
            + taps[2] * next_two * ahead[2:]
        )
        d_proj = jnp.concatenate(
            [d_bx * v_part, d_gated[r] * conv_out, d_bx * b_part], axis=1
        ).astype(BF)
        d_hidden_one = d_hidden_one + nt(d_proj, group[:width, : 3 * channels])
        mix_grads.append(
            jnp.concatenate([tn(hidden_one, d_proj).astype(BF), tn(d_mix, gated).astype(BF)], axis=1)
        )
    part_gain_one = jnp.sum(d_hidden_one * normed_one, axis=0)
    grad_input = d_resid + norm_back(d_hidden_one * gain_one, normed_one, scale_one)
    grad_input = reorder(grad_input, inverse, block)

    far = mix_grads[2].astype(F32) + swap(mix_grads[3], "tensor", 1).astype(F32)
    near = mix_grads[0].astype(F32) + swap(mix_grads[1], "tensor", 1).astype(F32)
    mix_sum = scatter_rows((near + swap(far.astype(BF), "tensor", 2).astype(F32)).astype(BF))

    conv_all = by_xor(jnp.stack(conv_parts), me_t)
    gain_parts = reorder(jnp.stack([part_gain_one, part_gain_two]), inverse, block)
    small = jnp.concatenate([gain_parts.reshape(2, 4, channels), conv_all.transpose(1, 0, 2)], axis=0)
    small = sum_all(small.reshape(small.shape[0], width))
    grad_conv = lax.dynamic_slice(small, (2, me_t * channels), (small.shape[0] - 2, channels))

    grad_in = mix_sum[:, : 3 * channels].reshape(block, 3, channels)
    grad_out = mix_sum[:, 3 * channels :].T
    grad_gu, grad_down = [], []
    for part, (lo, hi) in zip(ffn_grads, bounds):
        size = hi - lo
        grad_gu.append(part[:, : 2 * size].reshape(block, 2, size))
        grad_down.append(part[:, 2 * size :].T)
    return (
        block_out,
        grad_input,
        small[0],
        grad_in,
        grad_conv,
        grad_out,
        small[1],
        jnp.concatenate(grad_gu, axis=2),
        jnp.concatenate(grad_down, axis=0),
    )


def solution(mesh):
    return jax.shard_map(
        body,
        mesh=mesh,
        in_specs=(
            P(("dp", "tensor"), None),
            P("dp"),
            P(),
            P("dp", None, "tensor"),
            P(None, "tensor"),
            P("tensor", "dp"),
            P(),
            P("dp", None, "tensor"),
            P("tensor", "dp"),
            P(("dp", "tensor"), None),
        ),
        out_specs=(
            P(("dp", "tensor"), None),
            P(("dp", "tensor"), None),
            P(),
            P("dp", None, "tensor"),
            P(None, "tensor"),
            P("tensor", "dp"),
            P(),
            P("dp", None, "tensor"),
            P("tensor", "dp"),
        ),
        check_vma=False,
    )
```

time: 1220 us -> 546 us (0.45)
  waiting for transfers between devices: 945 us -> 199 us
  blocking collectives: 73.2 us -> 0 us
  starting transfers between devices: 5.91 us -> 52.1 us
  other arithmetic: 25.4 us -> 69.5 us
  Pallas kernels: 0 us -> 33 us
  local copies, waits for them, and re-layouts: 31.7 us -> 51 us
    reduce_scatter x7 -> x0, waiting for transfers between devices: 461 us -> none  [the longest x1 95.4 us: body(): lax.psum_scatter(grad_down_part, 'dp', scatter_dimension=1, tiled=True)]
    unnamed x16 -> x0, waiting for transfers between devices: 243 us -> none
    all_gather x7 -> x0, waiting for transfers between devices: 235 us -> none  [the longest x1 77.4 us: body(): lax.all_gather(gate_up_weight, 'dp', axis=0, tiled=True)]
    ppermute x2 -> x52, waiting for transfers between devices: 5.52 us -> 199 us  [the longest x32 139 us: swap(): return lax.ppermute(value, axis, [(i, i ^ bit) for i in range(peers)])]
    ppermute x2 -> x52, starting transfers between devices: 4.66 us -> 52.1 us  [the longest x18 25.3 us: ring(): lax.ppermute(value, axis, [(i, (i + by) % peers) for i in range(peers)])]
    psum x1 -> x0, blocking collectives: 40.1 us -> none  [body(): lax.psum((part_gain_one, part_gain_two, conv_spread), ('dp', 'tensor'))]
    all_gather x1 -> x0, blocking collectives: 33 us -> none  [body(): lax.all_gather(out_weight, 'dp', axis=1, tiled=True)]
    pallas_call x0 -> x6, Pallas kernels: none -> 33 us  [reorder(): pl.pallas_call(copy, out_shape=jax.ShapeDtypeStruct(value.shape, value.dt...]
  transfers between devices with their start and end apart: 17 -> 52, of which waited for: 17 -> 21; matrix products, arithmetic and copies ran while one was open for 10% -> 38% of each run, Pallas kernels for 0% -> 6%
where the time goes in v1:
time: 546 us; the launch traced here: 538 us
  waiting for transfers between devices  199 us (36%)
  matrix products  129 us (24%)
  other arithmetic  69.5 us (13%)
  starting transfers between devices  52.1 us (10%)
  local copies, waits for them, and re-layouts  51 us (9%)
  Pallas kernels  33 us (6%)
    ppermute x32, waiting for transfers between devices, swap(): return lax.ppermute(value, axis, [(i, i ^ bit) for i in range(peers)])  139 us
    ppermute x18, waiting for transfers between devices, ring(): lax.ppermute(value, axis, [(i, (i + by) % peers) for i in range(peers)])  59.5 us
    dot_general x12, matrix products, nn(): return jnp.dot(left, right, preferred_element_type=F32)  58.9 us
    dot_general x12, matrix products, nt(): lax.dot_general(left, right, (((1,), (1,)), ((), ())), preferred_element_...  38.1 us
    pallas_call x6, Pallas kernels, reorder(): pl.pallas_call(copy, out_shape=jax.ShapeDtypeStruct(value.shape, value.dt...  33 us
    dot_general x12, matrix products, tn(): lax.dot_general(left, right, (((0,), (0,)), ((), ())), preferred_element_...  32.2 us
    ppermute x18, starting transfers between devices, ring(): lax.ppermute(value, axis, [(i, (i + by) % peers) for i in range(peers)])  25.3 us
    ppermute x32, starting transfers between devices, swap(): return lax.ppermute(value, axis, [(i, i ^ bit) for i in range(peers)])  23.1 us
  transfers between devices with their start and end apart: 52, of which 21 were waited for; matrix products, arithmetic and copies ran while one was open for 38% of the time, Pallas kernels for 6%

profile of v1, /device:TPU:0, one launch (start us, length us, event | category | flops | bytes accessed | tf_op | source)
XLA Modules:
  0.0 538.2 jit_solution(7259013172214837624)
XLA Ops:
  2.0 3.4 concatenate.125
  15.1 2.6 collective-permute-start.12
  25.3 4.3 shard_map.224
  30.4 14.8 %collective-permute-done.1 = bf16[128,1024]{0,1:T(8,128)(2,1)S(1)} collective-permute-done((bf16[128,1024]{0,1:T(8,128)(2,1)S(1)}, bf16[128,1024]{0,1:T(8,128)(2,1)S(1)}, u32[]{:S(2)}, u32[]{:S(2)}) %collective-permute-start.1) | collective-permute-done | bytes 262176 | tf_op jit(solution)/shard_map/ppermute | solution.py:21
  45.7 5.9 %shard_map.226 = bf16[512,1024]{1,0:T(8,128)(2,1)} custom-call(s32[8]{0:T(128)} %fusion.101.order_ref, bf16[512,1024]{1,0:T(8,128)(2,1)} %in_ref.1), custom_call_target="tpu_custom_call" | custom-call | tf_op jit(solution)/shard_map/pallas_call | solution.py:59
  52.2 3.7 collective-permute-done.2
  59.1 6.7 %collective-permute-done.3 = bf16[128,1024]{0,1:T(8,128)(2,1)S(1)} collective-permute-done((bf16[128,1024]{0,1:T(8,128)(2,1)S(1)}, bf16[128,1024]{0,1:T(8,128)(2,1)S(1)}, u32[]{:S(2)}, u32[]{:S(2)}) %collective-permute-start.3) | collective-permute-done | bytes 262176 | tf_op jit(solution)/shard_map/ppermute | solution.py:21
  69.3 5.9 %shard_map.223 = bf16[528,1024]{1,0:T(8,128)(2,1)} custom-call(s32[8]{0:T(128)} %fusion.101.order_ref, bf16[528,1024]{1,0:T(8,128)(2,1)} %pad_maximum_fusion.13.in_ref), custom_call_target="tpu_custom_call" | custom-call | tf_op jit(solution)/shard_map/pallas_call | solution.py:59
  79.3 3.3 collective-permute-done.5
  100.0 7.1 %collective-permute-done.13 = bf16[128,1536]{0,1:T(8,128)(2,1)S(1)} collective-permute-done((bf16[128,1536]{0,1:T(8,128)(2,1)}, bf16[128,1536]{0,1:T(8,128)(2,1)S(1)}, u32[]{:S(2)}, u32[]{:S(2)}) %collective-permute-start.13) | collective-permute-done | bytes 393248 | tf_op jit(solution)/shard_map/ppermute | solution.py:21
  107.2 27.4 %collective-permute-done.7 = bf16[1040,1024]{1,0:T(8,128)(2,1)S(1)} collective-permute-done((bf16[1040,1024]{1,0:T(8,128)(2,1)}, bf16[1040,1024]{1,0:T(8,128)(2,1)S(1)}, u32[]{:S(2)}, u32[]{:S(2)}) %collective-permute-start.7) | collective-permute-done | bytes 2129952 | tf_op jit(solution)/shard_map/ppermute | solution.py:16
  148.7 12.8 %collective-permute-done.19 = bf16[128,1920]{0,1:T(8,128)(2,1)S(1)} collective-permute-done((bf16[128,1920]{0,1:T(8,128)(2,1)S(1)}, bf16[128,1920]{0,1:T(8,128)(2,1)S(1)}, u32[]{:S(2)}, u32[]{:S(2)}) %collective-permute-start.19) | collective-permute-done | bytes 491552 | tf_op jit(solution)/shard_map/ppermute | solution.py:21
  163.7 7.0 %collective-permute-done.10 = bf16[512,1024]{1,0:T(8,128)(2,1)S(1)} collective-permute-done((bf16[512,1024]{1,0:T(8,128)(2,1)S(1)}, bf16[512,1024]{1,0:T(8,128)(2,1)S(1)}, u32[]{:S(2)}, u32[]{:S(2)}) %collective-permute-start.10) | collective-permute-done | bytes 1048608 | tf_op jit(solution)/shard_map/ppermute | solution.py:16
  171.1 21.6 %collective-permute-done.26 = bf16[512,1024]{1,0:T(8,128)(2,1)S(1)} collective-permute-done((bf16[512,1024]{1,0:T(8,128)(2,1)S(1)}, bf16[512,1024]{1,0:T(8,128)(2,1)S(1)}, u32[]{:S(2)}, u32[]{:S(2)}) %collective-permute-start.26) | collective-permute-done | bytes 1048608 | tf_op jit(solution)/shard_map/ppermute | solution.py:16
  193.3 8.3 %collective-permute-done.21 = bf16[256,1920]{0,1:T(8,128)(2,1)S(1)} collective-permute-done((bf16[256,1920]{0,1:T(8,128)(2,1)S(1)}, bf16[256,1920]{0,1:T(8,128)(2,1)S(1)}, u32[]{:S(2)}, u32[]{:S(2)}) %collective-permute-start.21) | collective-permute-done | bytes 983072 | tf_op jit(solution)/shard_map/ppermute | solution.py:16
  203.7 10.2 %fusion.17 = f32[2048,1024]{0,1:T(8,128)} fusion(bf16[1024,1536]{0,1:T(8,128)(2,1)S(1)} %constant_dynamic-update-slice_fusion.12, bf16[512,1024]{1,0:T(8,128)(2,1)S(1)} %collective-permute-done.11, bf16[512,1024]{1,0:T(8,128)(2,1)S(1)} %collective-permute-done.10, bf16[512,1024]{1,0:T(8,128)(2,1)S(1)} %collective-permute-done.9, ...), kind=kOutput, calls=%fused_computation.71 | convolution fusion | flops 4311744512 | bytes 14680064 | tf_op jit(solution)/shard_map/dot_general | solution.py:31
  214.0 12.7 %multiply_convert_fusion.4 = (bf16[2048,512]{0,1:T(8,128)(2,1)S(1)}, bf16[2048,512]{0,1:T(8,128)(2,1)S(1)}, bf16[2048,512]{0,1:T(8,128)(2,1)S(1)}) fusion(f32[2048,1024]{0,1:T(8,128)} %fusion.17, bf16[1024,1536]{0,1:T(8,128)(2,1)S(1)} %constant_dynamic-update-slice_fusion.12, bf16[512,1024]{1,0:T(8,128)(2,1)S(1)} %collective-permute-done.27, ...), kind=kOutput, calls=%fused_computation.27 | convolution fusion | flops 2179989504 | bytes 19922944 | tf_op jit(solution)/shard_map/dot_general | solution.py:31
  226.7 2.6 convolution_convert_fusion.6
  229.3 4.5 fusion.15
  237.3 10.9 %fusion.5 = f32[2048,1280]{0,1:T(8,128)} fusion(bf16[1024,1920]{0,1:T(8,128)(2,1)S(1)} %copy-done.105, bf16[512,1024]{1,0:T(8,128)(2,1)S(1)} %collective-permute-done.11, bf16[512,1024]{1,0:T(8,128)(2,1)S(1)} %collective-permute-done.10, bf16[512,1024]{1,0:T(8,128)(2,1)S(1)} %collective-permute-done.9, bf16[512,1024]{1,0:T(8,128)(2,1)S(1)} %multiply_convert_fusion.7), kind=kOutput, calls=%fused_computation.42 | convolution fusion | flops 5385486336 | bytes 17301504 | tf_op jit(solution)/shard_map/dot_general | solution.py:31
  248.2 13.3 %multiply_convert_fusion.1 = (bf16[2048,640]{0,1:T(8,128)(2,1)}, bf16[2048,640]{0,1:T(8,128)(2,1)}, bf16[2048,640]{0,1:T(8,128)(2,1)}) fusion(f32[2048,1280]{0,1:T(8,128)} %fusion.5, bf16[1024,1920]{0,1:T(8,128)(2,1)S(1)} %copy-done.105, bf16[512,1024]{1,0:T(8,128)(2,1)S(1)} %copy-done.155, bf16[512,1024]{1,0:T(8,128)(2,1)S(1)} %copy-done.147, ...), kind=kOutput, calls=%fused_computation.11 | convolution fusion | flops 2720792576 | bytes 23855104 | tf_op jit(solution)/shard_map/dot_general | solution.py:31
  261.6 5.4 %fusion.37 = f32[2048,1024]{1,0:T(8,128)S(1)} fusion(bf16[2048,640]{0,1:T(8,128)(2,1)} %get-tuple-element.111, bf16[1024,1920]{0,1:T(8,128)(2,1)S(1)} %copy-done.105), kind=kOutput, calls=%fused_computation.102 | convolution fusion | flops 2684354560 | bytes 12320768 | tf_op jit(solution)/shard_map/dot_general | solution.py:39
  267.0 8.2 %fusion.2 = f32[2048,1024]{1,0:T(8,128)} fusion(bf16[2048,640]{0,1:T(8,128)(2,1)S(1)} %copy-done.164, bf16[2048,640]{0,1:T(8,128)(2,1)S(1)} %copy-done.163, bf16[1024,1920]{0,1:T(8,128)(2,1)S(1)} %copy-done.105), kind=kOutput, calls=%fused_computation.37 | convolution fusion | flops 5379194880 | bytes 16252928 | tf_op jit(solution)/shard_map/dot_general | solution.py:39
  275.3 3.8 convolution_convert_fusion.5
  279.1 9.3 %convolution_convert_fusion = bf16[1024,1280]{1,0:T(8,128)(2,1)S(1)} fusion(bf16[2048,640]{0,1:T(8,128)(2,1)} %get-tuple-element.108, bf16[2048,640]{0,1:T(8,128)(2,1)} %get-tuple-element.107, bf16[512,1024]{1,0:T(8,128)(2,1)} %copy-done.150, bf16[512,1024]{1,0:T(8,128)(2,1)S(1)} %copy-done.145, bf16[512,1024]{1,0:T(8,128)(2,1)} %copy-done.149, ...), kind=kOutput, calls=%fused_computation.33 | convolution fusion | flops 5397282816 | bytes 12058624 | tf_op jit(solution)/shard_map/dot_general | solution.py:35
  291.2 10.7 %fusion.136 = (bf16[2048,1024]{1,0:T(8,128)(2,1)S(1)}, f32[2048,1024]{1,0:T(8,128)}) fusion(f32[2048,1024]{1,0:T(8,128)} %fusion.2, bf16[1024,1536]{0,1:T(8,128)(2,1)S(1)} %copy-done.75, bf16[2048,512]{0,1:T(8,128)(2,1)} %copy-done.162, bf16[2048,512]{0,1:T(8,128)(2,1)} %copy-done.161), kind=kOutput, calls=%fused_computation.365 | convolution fusion | flops 4307550208 | bytes 27262976 | tf_op jit(solution)/shard_map/dot_general | solution.py:39
  304.2 6.0 %fusion.137 = (bf16[2048,1024]{1,0:T(8,128)(2,1)S(1)}, f32[2048,1024]{1,0:T(8,128)}) fusion(f32[2048,1024]{1,0:T(8,128)S(1)} %fusion.37, bf16[2048,512]{0,1:T(8,128)(2,1)S(1)} %copy-done.26, bf16[1024,1536]{0,1:T(8,128)(2,1)S(1)} %copy-done.75), kind=kOutput, calls=%fused_computation.366 | convolution fusion | flops 2151677952 | bytes 24117248 | tf_op jit(solution)/shard_map/dot_general | solution.py:39
  321.4 4.5 collective-permute-done.45
  328.8 4.9 collective-permute-done.48
  338.3 6.0 %collective-permute-done.30 = bf16[512,1024]{1,0:T(8,128)(2,1)S(1)} collective-permute-done((bf16[512,1024]{1,0:T(8,128)(2,1)S(1)}, bf16[512,1024]{1,0:T(8,128)(2,1)S(1)}, u32[]{:S(2)}, u32[]{:S(2)}) %collective-permute-start.30) | collective-permute-done | bytes 1048608 | tf_op jit(solution)/shard_map/ppermute | solution.py:16
  345.1 20.8 %collective-permute-done.24 = bf16[512,1024]{1,0:T(8,128)(2,1)S(1)} collective-permute-done((bf16[512,1024]{1,0:T(8,128)(2,1)S(1)}, bf16[512,1024]{1,0:T(8,128)(2,1)S(1)}, u32[]{:S(2)}, u32[]{:S(2)}) %collective-permute-start.24) | collective-permute-done | bytes 1048608 | tf_op jit(solution)/shard_map/ppermute | solution.py:16
  365.9 3.9 fusion.121
  379.9 2.5 multiply_reduce_fusion.13
  382.5 3.0 multiply_reduce_fusion.10
  390.3 6.0 %shard_map.225 = bf16[512,1024]{1,0:T(8,128)(2,1)} custom-call(s32[8]{0:T(128)} %fusion.95.order_ref, bf16[512,1024]{1,0:T(8,128)(2,1)} %get-tuple-element.117.in_ref), custom_call_target="tpu_custom_call" | custom-call | tf_op jit(solution)/shard_map/pallas_call | solution.py:59
  412.7 2.7 multiply_reduce_fusion.1
  415.9 4.5 shard_map.228
  422.0 2.4 convolution_convert_fusion.2
  430.9 4.6 add_convert_fusion.1
  443.2 6.3 %shard_map.227 = f32[512,1024]{1,0:T(8,128)} custom-call(s32[8]{0:T(128)} %fusion.95.order_ref, f32[512,1024]{1,0:T(8,128)} %multiply_add_fusion.in_ref), custom_call_target="tpu_custom_call" | custom-call | tf_op jit(solution)/shard_map/pallas_call | solution.py:59
  452.4 2.5 collective-permute-start.50
  457.8 24.3 %collective-permute-done.39 = bf16[1024,1024]{0,1:T(8,128)(2,1)} collective-permute-done((bf16[1024,1024]{0,1:T(8,128)(2,1)}, bf16[1024,1024]{0,1:T(8,128)(2,1)}, u32[]{:S(2)}, u32[]{:S(2)}) %collective-permute-start.39) | collective-permute-done | bytes 2097184 | tf_op jit(solution)/shard_map/ppermute | solution.py:16
  482.1 3.7 add_convert_fusion
  497.4 12.7 %collective-permute-done.40 = bf16[512,1024]{0,1:T(8,128)(2,1)} collective-permute-done((bf16[512,1024]{0,1:T(8,128)(2,1)}, bf16[512,1024]{0,1:T(8,128)(2,1)}, u32[]{:S(2)}, u32[]{:S(2)}) %collective-permute-start.40) | collective-permute-done | bytes 1048608 | tf_op jit(solution)/shard_map/ppermute | solution.py:16
  514.0 4.1 collective-permute-done.41
  519.2 2.7 collective-permute-start.42
  523.5 3.3 collective-permute-done.42
  527.9 3.4 collective-permute-start.43
  (582 shorter events, 172.1 us)
Async XLA Ops:
  8.9 59.3 %collective-permute-start = (bf16[16,1024]{1,0:T(8,128)(2,1)}, bf16[16,1024]{1,0:T(8,128)(2,1)S(1)}, u32[]{:S(2)}, u32[]{:S(2)}) collective-permute-start(bf16[16,1024]{1,0:T(8,128)(2,1)} %slice_multiply_fusion.24), channel_id=1, source_target_pairs={{0,1},{1,2},{2,3},{3,4},{4,5},{5,6},{6,7},{7,8},{8,9},{9,10},{10,1... | collective-permute-start | bytes 98312 | tf_op jit(solution)/shard_map/ppermute | solution.py:27
  15.1 75.6 %collective-permute-start.12 = (bf16[128,1536]{0,1:T(8,128)(2,1)}, bf16[128,1536]{0,1:T(8,128)(2,1)}, u32[]{:S(2)}, u32[]{:S(2)}) collective-permute-start(bf16[128,1536]{0,1:T(8,128)(2,1)} %get-tuple-element.134), channel_id=1, source_target_pairs={{0,8},{4,12},{8,16},{12,20},{16,24},{20,28},{24,0},{28,4},{1,9},{5... | collective-permute-start | bytes 1179656 | tf_op jit(solution)/shard_map/ppermute | solution.py:21
  19.9 75.2 %collective-permute-start.17 = (bf16[128,1920]{0,1:T(8,128)(2,1)}, bf16[128,1920]{0,1:T(8,128)(2,1)}, u32[]{:S(2)}, u32[]{:S(2)}) collective-permute-start(bf16[128,1920]{0,1:T(8,128)(2,1)} %get-tuple-element.132), channel_id=1, source_target_pairs={{0,8},{4,12},{8,16},{12,20},{16,24},{20,28},{24,0},{28,4},{1,9},{5... | collective-permute-start | bytes 1474568 | tf_op jit(solution)/shard_map/ppermute | solution.py:21
  22.5 22.7 %collective-permute-start.1 = (bf16[128,1024]{0,1:T(8,128)(2,1)S(1)}, bf16[128,1024]{0,1:T(8,128)(2,1)S(1)}, u32[]{:S(2)}, u32[]{:S(2)}) collective-permute-start(bf16[128,1024]{0,1:T(8,128)(2,1)S(1)} %get-tuple-element.144), channel_id=1, source_target_pairs={{0,8},{4,12},{8,16},{12,20},{16,24},{20,28},{24,0},{28,4},{1,9},{5... | collective-permute-start | bytes 786440 | tf_op jit(solution)/shard_map/ppermute | solution.py:21
  45.2 10.8 %collective-permute-start.2 = (bf16[128,1024]{0,1:T(8,128)(2,1)S(1)}, bf16[128,1024]{0,1:T(8,128)(2,1)S(1)}, u32[]{:S(2)}, u32[]{:S(2)}) collective-permute-start(bf16[128,1024]{0,1:T(8,128)(2,1)S(1)} %collective-permute-done.1), channel_id=1, source_target_pairs={{0,8},{4,12},{8,16},{12,20},{16,24},{20,28},{24,0},{28,4},{1,9},{5... | collective-permute-start | bytes 786440 | tf_op jit(solution)/shard_map/ppermute | solution.py:21
  55.9 9.9 %collective-permute-start.3 = (bf16[128,1024]{0,1:T(8,128)(2,1)S(1)}, bf16[128,1024]{0,1:T(8,128)(2,1)S(1)}, u32[]{:S(2)}, u32[]{:S(2)}) collective-permute-start(bf16[128,1024]{0,1:T(8,128)(2,1)S(1)} %collective-permute-done.2), channel_id=1, source_target_pairs={{0,8},{4,12},{8,16},{12,20},{16,24},{20,28},{24,0},{28,4},{1,9},{5... | collective-permute-start | bytes 786440 | tf_op jit(solution)/shard_map/ppermute | solution.py:21
  57.4 20.0 %collective-permute-start.4 = (bf16[256,1024]{0,1:T(8,128)(2,1)}, bf16[256,1024]{0,1:T(8,128)(2,1)}, u32[]{:S(2)}, u32[]{:S(2)}) collective-permute-start(bf16[256,1024]{0,1:T(8,128)(2,1)} %pad_maximum_fusion.27), channel_id=1, source_target_pairs={{0,4},{4,0},{8,12},{12,8},{16,20},{20,16},{24,28},{28,24},{1,5},{5... | collective-permute-start | bytes 1572872 | tf_op jit(solution)/shard_map/ppermute | solution.py:16
  66.7 16.0 %collective-permute-start.5 = (bf16[256,1024]{0,1:T(8,128)(2,1)}, bf16[256,1024]{0,1:T(8,128)(2,1)}, u32[]{:S(2)}, u32[]{:S(2)}) collective-permute-start(bf16[256,1024]{0,1:T(8,128)(2,1)} %pad_maximum_fusion.28), channel_id=1, source_target_pairs={{0,4},{4,0},{8,12},{12,8},{16,20},{20,16},{24,28},{28,24},{1,5},{5... | collective-permute-start | bytes 1572872 | tf_op jit(solution)/shard_map/ppermute | solution.py:16
  87.1 47.5 %collective-permute-start.7 = (bf16[1040,1024]{1,0:T(8,128)(2,1)}, bf16[1040,1024]{1,0:T(8,128)(2,1)S(1)}, u32[]{:S(2)}, u32[]{:S(2)}) collective-permute-start(bf16[1040,1024]{1,0:T(8,128)(2,1)} %copy.59), channel_id=1, source_target_pairs={{0,2},{1,3},{2,0},{3,1},{4,6},{5,7},{6,4},{7,5},{8,10},{9,11},{10,... | collective-permute-start | bytes 6389768 | tf_op jit(solution)/shard_map/ppermute | solution.py:16
  88.9 45.9 %collective-permute-start.6 = (bf16[1040,1024]{1,0:T(8,128)(2,1)}, bf16[1040,1024]{1,0:T(8,128)(2,1)S(1)}, u32[]{:S(2)}, u32[]{:S(2)}) collective-permute-start(bf16[1040,1024]{1,0:T(8,128)(2,1)} %copy.59), channel_id=1, source_target_pairs={{0,1},{1,0},{2,3},{3,2},{4,5},{5,4},{6,7},{7,6},{8,9},{9,8},{10,11... | collective-permute-start | bytes 6389768 | tf_op jit(solution)/shard_map/ppermute | solution.py:16
  92.5 70.4 %collective-permute-start.15 = (bf16[256,1536]{0,1:T(8,128)(2,1)S(1)}, bf16[256,1536]{0,1:T(8,128)(2,1)S(1)}, u32[]{:S(2)}, u32[]{:S(2)}) collective-permute-start(bf16[256,1536]{0,1:T(8,128)(2,1)S(1)} %pad_maximum_fusion.16), channel_id=1, source_target_pairs={{0,4},{4,0},{8,12},{12,8},{16,20},{20,16},{24,28},{28,24},{1,5},{5... | collective-permute-start | bytes 2359304 | tf_op jit(solution)/shard_map/ppermute | solution.py:16
  93.9 13.2 %collective-permute-start.13 = (bf16[128,1536]{0,1:T(8,128)(2,1)}, bf16[128,1536]{0,1:T(8,128)(2,1)S(1)}, u32[]{:S(2)}, u32[]{:S(2)}) collective-permute-start(bf16[128,1536]{0,1:T(8,128)(2,1)} %collective-permute-done.12), channel_id=1, source_target_pairs={{0,8},{4,12},{8,16},{12,20},{16,24},{20,28},{24,0},{28,4},{1,9},{5... | collective-permute-start | bytes 1179656 | tf_op jit(solution)/shard_map/ppermute | solution.py:21
  96.3 67.4 %collective-permute-start.20 = (bf16[256,1920]{0,1:T(8,128)(2,1)S(1)}, bf16[256,1920]{0,1:T(8,128)(2,1)S(1)}, u32[]{:S(2)}, u32[]{:S(2)}) collective-permute-start(bf16[256,1920]{0,1:T(8,128)(2,1)S(1)} %pad_maximum_fusion.14), channel_id=1, source_target_pairs={{0,4},{4,0},{8,12},{12,8},{16,20},{20,16},{24,28},{28,24},{1,5},{5... | collective-permute-start | bytes 2949128 | tf_op jit(solution)/shard_map/ppermute | solution.py:16
  107.2 38.9 %collective-permute-start.18 = (bf16[128,1920]{0,1:T(8,128)(2,1)}, bf16[128,1920]{0,1:T(8,128)(2,1)S(1)}, u32[]{:S(2)}, u32[]{:S(2)}) collective-permute-start(bf16[128,1920]{0,1:T(8,128)(2,1)} %collective-permute-done.17), channel_id=1, source_target_pairs={{0,8},{4,12},{8,16},{12,20},{16,24},{20,28},{24,0},{28,4},{1,9},{5... | collective-permute-start | bytes 1474568 | tf_op jit(solution)/shard_map/ppermute | solution.py:21
  134.5 13.6 %collective-permute-start.14 = (bf16[128,1536]{0,1:T(8,128)(2,1)S(1)}, bf16[128,1536]{0,1:T(8,128)(2,1)S(1)}, u32[]{:S(2)}, u32[]{:S(2)}) collective-permute-start(bf16[128,1536]{0,1:T(8,128)(2,1)S(1)} %collective-permute-done.13), channel_id=1, source_target_pairs={{0,8},{4,12},{8,16},{12,20},{16,24},{20,28},{24,0},{28,4},{1,9},{5... | collective-permute-start | bytes 1179656 | tf_op jit(solution)/shard_map/ppermute | solution.py:21
  144.7 26.0 %collective-permute-start.10 = (bf16[512,1024]{1,0:T(8,128)(2,1)S(1)}, bf16[512,1024]{1,0:T(8,128)(2,1)S(1)}, u32[]{:S(2)}, u32[]{:S(2)}) collective-permute-start(bf16[512,1024]{1,0:T(8,128)(2,1)S(1)} %multiply_convert_fusion.7), channel_id=1, source_target_pairs={{0,2},{1,3},{2,0},{3,1},{4,6},{5,7},{6,4},{7,5},{8,10},{9,11},{10,... | collective-permute-start | bytes 3145736 | tf_op jit(solution)/shard_map/ppermute | solution.py:16
  146.1 15.4 %collective-permute-start.19 = (bf16[128,1920]{0,1:T(8,128)(2,1)S(1)}, bf16[128,1920]{0,1:T(8,128)(2,1)S(1)}, u32[]{:S(2)}, u32[]{:S(2)}) collective-permute-start(bf16[128,1920]{0,1:T(8,128)(2,1)S(1)} %collective-permute-done.18), channel_id=1, source_target_pairs={{0,8},{4,12},{8,16},{12,20},{16,24},{20,28},{24,0},{28,4},{1,9},{5... | collective-permute-start | bytes 1474568 | tf_op jit(solution)/shard_map/ppermute | solution.py:21
  148.1 44.6 %collective-permute-start.26 = (bf16[512,1024]{1,0:T(8,128)(2,1)S(1)}, bf16[512,1024]{1,0:T(8,128)(2,1)S(1)}, u32[]{:S(2)}, u32[]{:S(2)}) collective-permute-start(bf16[512,1024]{1,0:T(8,128)(2,1)S(1)} %copy-done.35), channel_id=1, source_target_pairs={{0,2},{1,3},{2,0},{3,1},{4,6},{5,7},{6,4},{7,5},{8,10},{9,11},{10,... | collective-permute-start | bytes 3145736 | tf_op jit(solution)/shard_map/ppermute | solution.py:16
  161.5 31.2 %collective-permute-start.16 = (bf16[256,1536]{0,1:T(8,128)(2,1)S(1)}, bf16[256,1536]{0,1:T(8,128)(2,1)S(1)}, u32[]{:S(2)}, u32[]{:S(2)}) collective-permute-start(bf16[256,1536]{0,1:T(8,128)(2,1)S(1)} %pad_maximum_fusion.17), channel_id=1, source_target_pairs={{0,4},{4,0},{8,12},{12,8},{16,20},{20,16},{24,28},{28,24},{1,5},{5... | collective-permute-start | bytes 2359304 | tf_op jit(solution)/shard_map/ppermute | solution.py:16
  162.9 38.7 %collective-permute-start.21 = (bf16[256,1920]{0,1:T(8,128)(2,1)S(1)}, bf16[256,1920]{0,1:T(8,128)(2,1)S(1)}, u32[]{:S(2)}, u32[]{:S(2)}) collective-permute-start(bf16[256,1920]{0,1:T(8,128)(2,1)S(1)} %pad_maximum_fusion.15), channel_id=1, source_target_pairs={{0,4},{4,0},{8,12},{12,8},{16,20},{20,16},{24,28},{28,24},{1,5},{5... | collective-permute-start | bytes 2949128 | tf_op jit(solution)/shard_map/ppermute | solution.py:16
  163.7 38.0 %collective-permute-start.9 = (bf16[512,1024]{1,0:T(8,128)(2,1)S(1)}, bf16[512,1024]{1,0:T(8,128)(2,1)S(1)}, u32[]{:S(2)}, u32[]{:S(2)}) collective-permute-start(bf16[512,1024]{1,0:T(8,128)(2,1)S(1)} %multiply_convert_fusion.7), channel_id=1, source_target_pairs={{0,1},{1,0},{2,3},{3,2},{4,5},{5,4},{6,7},{7,6},{8,9},{9,8},{10,11... | collective-permute-start | bytes 3145736 | tf_op jit(solution)/shard_map/ppermute | solution.py:16
  170.7 33.0 %collective-permute-start.11 = (bf16[512,1024]{1,0:T(8,128)(2,1)S(1)}, bf16[512,1024]{1,0:T(8,128)(2,1)S(1)}, u32[]{:S(2)}, u32[]{:S(2)}) collective-permute-start(bf16[512,1024]{1,0:T(8,128)(2,1)S(1)} %collective-permute-done.10), channel_id=1, source_target_pairs={{0,1},{1,0},{2,3},{3,2},{4,5},{5,4},{6,7},{7,6},{8,9},{9,8},{10,11... | collective-permute-start | bytes 3145736 | tf_op jit(solution)/shard_map/ppermute | solution.py:16
  192.7 21.2 %collective-permute-start.25 = (bf16[512,1024]{1,0:T(8,128)(2,1)S(1)}, bf16[512,1024]{1,0:T(8,128)(2,1)S(1)}, u32[]{:S(2)}, u32[]{:S(2)}) collective-permute-start(bf16[512,1024]{1,0:T(8,128)(2,1)S(1)} %copy-done.35), channel_id=1, source_target_pairs={{0,1},{1,0},{2,3},{3,2},{4,5},{5,4},{6,7},{7,6},{8,9},{9,8},{10,11... | collective-permute-start | bytes 3145736 | tf_op jit(solution)/shard_map/ppermute | solution.py:16
  192.7 21.2 %collective-permute-start.27 = (bf16[512,1024]{1,0:T(8,128)(2,1)S(1)}, bf16[512,1024]{1,0:T(8,128)(2,1)S(1)}, u32[]{:S(2)}, u32[]{:S(2)}) collective-permute-start(bf16[512,1024]{1,0:T(8,128)(2,1)S(1)} %collective-permute-done.26), channel_id=1, source_target_pairs={{0,1},{1,0},{2,3},{3,2},{4,5},{5,4},{6,7},{7,6},{8,9},{9,8},{10,11... | collective-permute-start | bytes 3145736 | tf_op jit(solution)/shard_map/ppermute | solution.py:16
  235.8 77.1 %collective-permute-start.44 = (bf16[512,1536]{0,1:T(8,128)(2,1)}, bf16[512,1536]{0,1:T(8,128)(2,1)}, u32[]{:S(2)}, u32[]{:S(2)}) collective-permute-start(bf16[512,1536]{0,1:T(8,128)(2,1)} %fusion.19), channel_id=1, source_target_pairs={{0,4},{4,0},{8,12},{12,8},{16,20},{20,16},{24,28},{28,24},{1,5},{5... | collective-permute-start | bytes 4718600 | tf_op jit(solution)/shard_map/ppermute | solution.py:16
  289.9 43.7 %collective-permute-start.48 = (bf16[512,1920]{1,0:T(8,128)(2,1)}, bf16[512,1920]{1,0:T(8,128)(2,1)}, u32[]{:S(2)}, u32[]{:S(2)}) collective-permute-start(bf16[512,1920]{1,0:T(8,128)(2,1)} %fusion.14), channel_id=1, source_target_pairs={{0,4},{4,0},{8,12},{12,8},{16,20},{20,16},{24,28},{28,24},{1,5},{5... | collective-permute-start | bytes 5898248 | tf_op jit(solution)/shard_map/ppermute | solution.py:16
  303.4 11.0 %collective-permute-start.29 = (bf16[512,1024]{1,0:T(8,128)(2,1)}, bf16[512,1024]{1,0:T(8,128)(2,1)}, u32[]{:S(2)}, u32[]{:S(2)}) collective-permute-start(bf16[512,1024]{1,0:T(8,128)(2,1)} %get-tuple-element.114), channel_id=1, source_target_pairs={{0,1},{1,0},{2,3},{3,2},{4,5},{5,4},{6,7},{7,6},{8,9},{9,8},{10,11... | collective-permute-start | bytes 3145736 | tf_op jit(solution)/shard_map/ppermute | solution.py:16
  311.7 6.4 %collective-permute-start.23 = (bf16[512,1024]{1,0:T(8,128)(2,1)}, bf16[512,1024]{1,0:T(8,128)(2,1)}, u32[]{:S(2)}, u32[]{:S(2)}) collective-permute-start(bf16[512,1024]{1,0:T(8,128)(2,1)} %get-tuple-element.116), channel_id=1, source_target_pairs={{0,1},{1,0},{2,3},{3,2},{4,5},{5,4},{6,7},{7,6},{8,9},{9,8},{10,11... | collective-permute-start | bytes 3145736 | tf_op jit(solution)/shard_map/ppermute | solution.py:16
  312.4 24.4 %collective-permute-start.28 = (bf16[512,1024]{1,0:T(8,128)(2,1)}, bf16[512,1024]{1,0:T(8,128)(2,1)S(1)}, u32[]{:S(2)}, u32[]{:S(2)}) collective-permute-start(bf16[512,1024]{1,0:T(8,128)(2,1)} %get-tuple-element.113), channel_id=1, source_target_pairs={{0,1},{1,0},{2,3},{3,2},{4,5},{5,4},{6,7},{7,6},{8,9},{9,8},{10,11... | collective-permute-start | bytes 3145736 | tf_op jit(solution)/shard_map/ppermute | solution.py:16
  312.9 32.2 %collective-permute-start.22 = (bf16[512,1024]{1,0:T(8,128)(2,1)}, bf16[512,1024]{1,0:T(8,128)(2,1)S(1)}, u32[]{:S(2)}, u32[]{:S(2)}) collective-permute-start(bf16[512,1024]{1,0:T(8,128)(2,1)} %get-tuple-element.115), channel_id=1, source_target_pairs={{0,1},{1,0},{2,3},{3,2},{4,5},{5,4},{6,7},{7,6},{8,9},{9,8},{10,11... | collective-permute-start | bytes 3145736 | tf_op jit(solution)/shard_map/ppermute | solution.py:16
  314.4 11.5 %collective-permute-start.45 = (bf16[128,1536]{0,1:T(8,128)(2,1)S(1)}, bf16[128,1536]{0,1:T(8,128)(2,1)S(1)}, u32[]{:S(2)}, u32[]{:S(2)}) collective-permute-start(bf16[128,1536]{0,1:T(8,128)(2,1)S(1)} %add_convert_fusion.7), channel_id=1, source_target_pairs={{0,24},{4,28},{8,0},{12,4},{16,8},{20,12},{24,16},{28,20},{1,25},{... | collective-permute-start | bytes 1179656 | tf_op jit(solution)/shard_map/ppermute | solution.py:21
  318.2 26.1 %collective-permute-start.30 = (bf16[512,1024]{1,0:T(8,128)(2,1)S(1)}, bf16[512,1024]{1,0:T(8,128)(2,1)S(1)}, u32[]{:S(2)}, u32[]{:S(2)}) collective-permute-start(bf16[512,1024]{1,0:T(8,128)(2,1)S(1)} %fusion.8), channel_id=1, source_target_pairs={{0,2},{1,3},{2,0},{3,1},{4,6},{5,7},{6,4},{7,5},{8,10},{9,11},{10,... | collective-permute-start | bytes 3145736 | tf_op jit(solution)/shard_map/ppermute | solution.py:16
  325.9 40.0 %collective-permute-start.24 = (bf16[512,1024]{1,0:T(8,128)(2,1)S(1)}, bf16[512,1024]{1,0:T(8,128)(2,1)S(1)}, u32[]{:S(2)}, u32[]{:S(2)}) collective-permute-start(bf16[512,1024]{1,0:T(8,128)(2,1)S(1)} %fusion.10), channel_id=1, source_target_pairs={{0,2},{1,3},{2,0},{3,1},{4,6},{5,7},{6,4},{7,5},{8,10},{9,11},{10,... | collective-permute-start | bytes 3145736 | tf_op jit(solution)/shard_map/ppermute | solution.py:16
  333.7 121.3 %collective-permute-start.46 = (bf16[128,1536]{0,1:T(8,128)(2,1)}, bf16[128,1536]{0,1:T(8,128)(2,1)}, u32[]{:S(2)}, u32[]{:S(2)}) collective-permute-start(bf16[128,1536]{0,1:T(8,128)(2,1)} %add_convert_fusion.6), channel_id=1, source_target_pairs={{0,24},{4,28},{8,0},{12,4},{16,8},{20,12},{24,16},{28,20},{1,25},{... | collective-permute-start | bytes 1179656 | tf_op jit(solution)/shard_map/ppermute | solution.py:21
  336.8 114.0 %collective-permute-start.49 = (bf16[128,1920]{1,0:T(8,128)(2,1)}, bf16[128,1920]{1,0:T(8,128)(2,1)}, u32[]{:S(2)}, u32[]{:S(2)}) collective-permute-start(bf16[128,1920]{1,0:T(8,128)(2,1)} %add_convert_fusion.4), channel_id=1, source_target_pairs={{0,24},{4,28},{8,0},{12,4},{16,8},{20,12},{24,16},{28,20},{1,25},{... | collective-permute-start | bytes 1474568 | tf_op jit(solution)/shard_map/ppermute | solution.py:21
  389.0 7.4 %collective-permute-start.31 = (f32[4,2,256]{2,1,0:T(2,128)S(1)}, f32[4,2,256]{2,1,0:T(2,128)S(1)}, u32[]{:S(2)}, u32[]{:S(2)}) collective-permute-start(f32[4,2,256]{2,1,0:T(2,128)S(1)} %bitcast.163), channel_id=1, source_target_pairs={{1,0},{2,1},{3,2},{4,3},{5,4},{6,5},{7,6},{8,7},{9,8},{10,9},{11,1... | collective-permute-start | bytes 24584 | tf_op jit(solution)/shard_map/ppermute | solution.py:27
  406.0 24.9 %collective-permute-start.38 = (bf16[1024,1024]{0,1:T(8,128)(2,1)}, bf16[1024,1024]{0,1:T(8,128)(2,1)}, u32[]{:S(2)}, u32[]{:S(2)}) collective-permute-start(bf16[1024,1024]{0,1:T(8,128)(2,1)} %pad_maximum_fusion.9), channel_id=1, source_target_pairs={{0,1},{1,0},{2,3},{3,2},{4,5},{5,4},{6,7},{7,6},{8,9},{9,8},{10,11... | collective-permute-start | bytes 6291464 | tf_op jit(solution)/shard_map/ppermute | solution.py:16
  428.1 29.7 %collective-permute-start.37 = (bf16[1024,1024]{0,1:T(8,128)(2,1)}, bf16[1024,1024]{0,1:T(8,128)(2,1)}, u32[]{:S(2)}, u32[]{:S(2)}) collective-permute-start(bf16[1024,1024]{0,1:T(8,128)(2,1)} %pad_maximum_fusion.8), channel_id=1, source_target_pairs={{0,1},{1,0},{2,3},{3,2},{4,5},{5,4},{6,7},{7,6},{8,9},{9,8},{10,11... | collective-permute-start | bytes 6291464 | tf_op jit(solution)/shard_map/ppermute | solution.py:16
  429.7 6.7 %collective-permute-start.34 = (f32[5,1024]{1,0:T(8,128)S(1)}, f32[5,1024]{1,0:T(8,128)S(1)}, u32[]{:S(2)}, u32[]{:S(2)}) collective-permute-start(f32[5,1024]{1,0:T(8,128)S(1)} %add.346), channel_id=1, source_target_pairs={{0,4},{4,0},{8,12},{12,8},{16,20},{20,16},{24,28},{28,24},{1,5},{5... | collective-permute-start | bytes 61448 | tf_op jit(solution)/shard_map/ppermute | solution.py:16
  435.5 46.6 %collective-permute-start.39 = (bf16[1024,1024]{0,1:T(8,128)(2,1)}, bf16[1024,1024]{0,1:T(8,128)(2,1)}, u32[]{:S(2)}, u32[]{:S(2)}) collective-permute-start(bf16[1024,1024]{0,1:T(8,128)(2,1)} %add_convert_fusion.1), channel_id=1, source_target_pairs={{0,2},{1,3},{2,0},{3,1},{4,6},{5,7},{6,4},{7,5},{8,10},{9,11},{10,... | collective-permute-start | bytes 6291464 | tf_op jit(solution)/shard_map/ppermute | solution.py:16
  440.3 9.2 %collective-permute-start.36 = (f32[5,1024]{1,0:T(8,128)S(1)}, f32[5,1024]{1,0:T(8,128)S(1)}, u32[]{:S(2)}, u32[]{:S(2)}) collective-permute-start(f32[5,1024]{1,0:T(8,128)S(1)} %add.348), channel_id=1, source_target_pairs={{0,16},{4,20},{8,24},{12,28},{16,0},{20,4},{24,8},{28,12},{1,17},{... | collective-permute-start | bytes 61448 | tf_op jit(solution)/shard_map/ppermute | solution.py:16
  452.4 35.0 %collective-permute-start.50 = (bf16[128,1920]{1,0:T(8,128)(2,1)S(1)}, bf16[128,1920]{1,0:T(8,128)(2,1)S(1)}, u32[]{:S(2)}, u32[]{:S(2)}) collective-permute-start(bf16[128,1920]{1,0:T(8,128)(2,1)S(1)} %add_convert_fusion.3), channel_id=1, source_target_pairs={{0,24},{4,28},{8,0},{12,4},{16,8},{20,12},{24,16},{28,20},{1,25},{... | collective-permute-start | bytes 1474568 | tf_op jit(solution)/shard_map/ppermute | solution.py:21
  456.3 35.4 %collective-permute-start.47 = (bf16[128,1536]{0,1:T(8,128)(2,1)S(1)}, bf16[128,1536]{0,1:T(8,128)(2,1)S(1)}, u32[]{:S(2)}, u32[]{:S(2)}) collective-permute-start(bf16[128,1536]{0,1:T(8,128)(2,1)S(1)} %add_convert_fusion.5), channel_id=1, source_target_pairs={{0,24},{4,28},{8,0},{12,4},{16,8},{20,12},{24,16},{28,20},{1,25},{... | collective-permute-start | bytes 1179656 | tf_op jit(solution)/shard_map/ppermute | solution.py:21
  486.9 23.2 %collective-permute-start.40 = (bf16[512,1024]{0,1:T(8,128)(2,1)}, bf16[512,1024]{0,1:T(8,128)(2,1)}, u32[]{:S(2)}, u32[]{:S(2)}) collective-permute-start(bf16[512,1024]{0,1:T(8,128)(2,1)} %slice.770), channel_id=1, source_target_pairs={{0,4},{4,0},{8,12},{12,8},{16,20},{20,16},{24,28},{28,24},{1,5},{5... | collective-permute-start | bytes 3145736 | tf_op jit(solution)/shard_map/ppermute | solution.py:16
  490.2 22.4 %collective-permute-start.51 = (bf16[128,1920]{1,0:T(8,128)(2,1)}, bf16[128,1920]{1,0:T(8,128)(2,1)}, u32[]{:S(2)}, u32[]{:S(2)}) collective-permute-start(bf16[128,1920]{1,0:T(8,128)(2,1)} %add_convert_fusion.2), channel_id=1, source_target_pairs={{0,24},{4,28},{8,0},{12,4},{16,8},{20,12},{24,16},{28,20},{1,25},{... | collective-permute-start | bytes 1474568 | tf_op jit(solution)/shard_map/ppermute | solution.py:21
  511.3 6.8 %collective-permute-start.41 = (bf16[128,1024]{0,1:T(8,128)(2,1)S(1)}, bf16[128,1024]{0,1:T(8,128)(2,1)S(1)}, u32[]{:S(2)}, u32[]{:S(2)}) collective-permute-start(bf16[128,1024]{0,1:T(8,128)(2,1)S(1)} %add_convert_fusion.10), channel_id=1, source_target_pairs={{0,24},{4,28},{8,0},{12,4},{16,8},{20,12},{24,16},{28,20},{1,25},{... | collective-permute-start | bytes 786440 | tf_op jit(solution)/shard_map/ppermute | solution.py:21
  519.2 7.6 %collective-permute-start.42 = (bf16[128,1024]{0,1:T(8,128)(2,1)S(1)}, bf16[128,1024]{0,1:T(8,128)(2,1)S(1)}, u32[]{:S(2)}, u32[]{:S(2)}) collective-permute-start(bf16[128,1024]{0,1:T(8,128)(2,1)S(1)} %add_convert_fusion.9), channel_id=1, source_target_pairs={{0,24},{4,28},{8,0},{12,4},{16,8},{20,12},{24,16},{28,20},{1,25},{... | collective-permute-start | bytes 786440 | tf_op jit(solution)/shard_map/ppermute | solution.py:21
  527.9 7.3 %collective-permute-start.43 = (bf16[128,1024]{0,1:T(8,128)(2,1)S(1)}, bf16[128,1024]{0,1:T(8,128)(2,1)S(1)}, u32[]{:S(2)}, u32[]{:S(2)}) collective-permute-start(bf16[128,1024]{0,1:T(8,128)(2,1)S(1)} %add_convert_fusion.8), channel_id=1, source_target_pairs={{0,24},{4,28},{8,0},{12,4},{16,8},{20,12},{24,16},{28,20},{1,25},{... | collective-permute-start | bytes 786440 | tf_op jit(solution)/shard_map/ppermute | solution.py:21
  (169 other events, 1463.3 us)
